TPU v7x, 256 devices: a whole 4x4x8 slice. The times are simulated.
256 devices in a mesh: ctx: 32 (over z, y), ch: 8 (over x, core).
Axes of the slice: x: 4, y: 4, z: 8, core: 2. Of those that a mesh axis runs over, the one named last changes fastest.
Arguments:
- queries: bfloat16 [8192, 4096], P('ctx', 'ch'), may hold values from -6 to 6
- keys: bfloat16 [8192, 4096], P('ctx', 'ch'), may hold values from -6 to 6
- values: bfloat16 [8192, 4096], P('ctx', 'ch'), may hold values from -6 to 6
- long_filter: float32 [8192, 4096], P('ctx', 'ch'), may hold values from -1.05 to 1.05
- short_filters: float32 [3, 3, 4096], P(None, None, 'ch'), may hold values from -3.6 to 3.6
- skip: float32 [4096], P('ch'), may hold values from -1 to 1
- w_out: bfloat16 [4096, 8192], P('ch'), may hold values from -0.09375 to 0.09375
- d_out: bfloat16 [8192, 8192], P('ctx', 'ch'), may hold values from -6 to 6
Outputs:
- d_queries: bfloat16 [8192, 4096], P('ctx', 'ch')
- d_keys: bfloat16 [8192, 4096], P('ctx', 'ch')
- d_values: bfloat16 [8192, 4096], P('ctx', 'ch')
- d_long: float32 [8192, 4096], P('ctx', 'ch')
- d_short: float32 [3, 3, 4096], P(None, None, 'ch')
- d_skip: float32 [4096], P('ch')
All inputs are finite; a program needn't handle non-finite values.
Results may differ from a plain program's by a relative error of at most 0.0049.
Values may be sent and summed in bfloat16 or wider, within the bound.
No kernel may reach another device: no remote copies, remote signals or barrier semaphores. Data moves between devices by JAX's collectives and lax.ppermute only.
A program may use at most 128 MiB of HBM per device.

v0:
```python
import math
import jax
import jax.numpy as jnp
from jax import lax
from jax.sharding import PartitionSpec as P


def passed_along(block, axis, distance):
    devices = range(lax.axis_size(axis))
    route = [(i - distance, i) for i in devices if i - distance in devices]
    return lax.ppermute(block, axis, route)


def phases(left_index, right_index, modulus):
    product = left_index[:, None] * right_index[None, :] % modulus
    angle = product.astype(jnp.float32) * (2.0 * math.pi / modulus)
    return (jnp.cos(angle), jnp.sin(angle))


def mat_apply(table, data, form):
    return jnp.einsum(form, table, data, precision=lax.Precision.HIGHEST)


def forward_full(regrouped, ctx_size, position, block_len, total_len):
    seq_rows = ctx_size * block_len
    coarse = jnp.arange(ctx_size, dtype=jnp.int32)
    freq_coarse = jnp.arange(2 * ctx_size, dtype=jnp.int32)
    coarse_cos, coarse_sin = phases(freq_coarse, coarse, 2 * ctx_size)
    first_real = mat_apply(coarse_cos, regrouped, "ka,sabc->skbc")
    first_imag = -mat_apply(coarse_sin, regrouped, "ka,sabc->skbc")
    fine_global = position * block_len + jnp.arange(block_len, dtype=jnp.int32)
    twist_cos, twist_sin = phases(freq_coarse, fine_global, total_len)
    twist_cos = twist_cos[None, :, :, None]
    twist_sin = twist_sin[None, :, :, None]
    second_real = first_real * twist_cos + first_imag * twist_sin
    second_imag = first_imag * twist_cos - first_real * twist_sin
    moved = lax.all_to_all(
        jnp.stack([second_real, second_imag], axis=1),
        "ctx",
        split_axis=2,
        concat_axis=3,
        tiled=True,
    )
    fine_index = jnp.arange(seq_rows, dtype=jnp.int32)
    fine_cos, fine_sin = phases(fine_index, fine_index, seq_rows)
    moved_real = moved[:, 0]
    moved_imag = moved[:, 1]
    spec_real = mat_apply(fine_cos, moved_real, "kb,smbc->smkc") + mat_apply(
        fine_sin, moved_imag, "kb,smbc->smkc"
    )
    spec_imag = mat_apply(fine_cos, moved_imag, "kb,smbc->smkc") - mat_apply(
        fine_sin, moved_real, "kb,smbc->smkc"
    )
    return (spec_real, spec_imag)


def inverse_full(spec_real, spec_imag, ctx_size, position, block_len, total_len):
    seq_rows = spec_real.shape[2]
    fine_index = jnp.arange(seq_rows, dtype=jnp.int32)
    fine_cos, fine_sin = phases(fine_index, fine_index, seq_rows)
    back_real = mat_apply(fine_cos, spec_real, "bk,smkc->smbc") - mat_apply(
        fine_sin, spec_imag, "bk,smkc->smbc"
    )
    back_imag = mat_apply(fine_cos, spec_imag, "bk,smkc->smbc") + mat_apply(
        fine_sin, spec_real, "bk,smkc->smbc"
    )
    returned = lax.all_to_all(
        jnp.stack([back_real, back_imag], axis=1), "ctx", split_axis=3, concat_axis=2, tiled=True
    )
    part_real = returned[:, 0]
    part_imag = returned[:, 1]
    freq_coarse = jnp.arange(2 * ctx_size, dtype=jnp.int32)
    fine_global = position * block_len + jnp.arange(block_len, dtype=jnp.int32)
    twist_cos, twist_sin = phases(freq_coarse, fine_global, total_len)
    twist_cos = twist_cos[None, :, :, None]
    twist_sin = twist_sin[None, :, :, None]
    turned_real = part_real * twist_cos - part_imag * twist_sin
    turned_imag = part_imag * twist_cos + part_real * twist_sin
    coarse = jnp.arange(ctx_size, dtype=jnp.int32)
    coarse_cos, coarse_sin = phases(coarse, freq_coarse, 2 * ctx_size)
    result_real = mat_apply(coarse_cos, turned_real, "ak,skbc->sabc") - mat_apply(
        coarse_sin, turned_imag, "ak,skbc->sabc"
    )
    result_imag = mat_apply(coarse_cos, turned_imag, "ak,skbc->sabc") + mat_apply(
        coarse_sin, turned_real, "ak,skbc->sabc"
    )
    return (result_real / total_len, result_imag / total_len)


def per_device(queries, keys, values, long_filter, short_filters, skip, w_out, d_out):
    ctx_size = lax.axis_size("ctx")
    position = lax.axis_index("ctx")
    seq_rows = queries.shape[0]
    width = queries.shape[1]
    block_len = seq_rows // ctx_size
    total_len = 2 * ctx_size * seq_rows
    tap_count = short_filters.shape[1]
    rim_width = tap_count - 1
    streams = jnp.stack([queries, keys, values])
    before = passed_along(streams[:, seq_rows - rim_width :, :], "ctx", 1)
    extended = jnp.concatenate([before, streams], axis=1).astype(jnp.float32)
    filtered = jnp.zeros((3, seq_rows, width), jnp.float32)
    for j in range(tap_count):
        filtered = (
            filtered
            + short_filters[:, j, None, :]
            * extended[:, rim_width - j : rim_width - j + seq_rows, :]
        )
    mixed = filtered[1] * filtered[2]
    accumulated = lax.dot_general(
        lax.all_gather(d_out, "ch", axis=1, tiled=True),
        w_out,
        (((1,), (1,)), ((), ())),
        preferred_element_type=jnp.float32,
    )
    grad_o = lax.optimization_barrier(accumulated.astype(jnp.bfloat16)).astype(jnp.float32)
    grad_y = grad_o * filtered[0]
    signals = jnp.stack([mixed, long_filter, grad_y])
    regrouped = lax.all_to_all(signals[:, None], "ctx", split_axis=2, concat_axis=1, tiled=True)
    spec_real, spec_imag = forward_full(regrouped, ctx_size, position, block_len, total_len)
    mix_re, mix_im = (spec_real[0], spec_imag[0])
    fil_re, fil_im = (spec_real[1], spec_imag[1])
    grad_re, grad_im = (spec_real[2], spec_imag[2])
    out_re = mix_re * fil_re - mix_im * fil_im
    out_im = mix_re * fil_im + mix_im * fil_re
    back_re = grad_re * fil_re + grad_im * fil_im
    back_im = grad_im * fil_re - grad_re * fil_im
    corr_re = grad_re * mix_re + grad_im * mix_im
    corr_im = grad_im * mix_re - grad_re * mix_im
    result_real, result_imag = inverse_full(
        jnp.stack([out_re, back_re, corr_re]),
        jnp.stack([out_im, back_im, corr_im]),
        ctx_size,
        position,
        block_len,
        total_len,
    )
    timed = lax.all_to_all(result_real, "ctx", split_axis=1, concat_axis=2, tiled=True).reshape(
        3, seq_rows, width
    )
    conv_y = timed[0]
    conv_back = timed[1]
    d_long = timed[2]
    y_full = conv_y + skip[None, :] * mixed
    grad_mixed = conv_back + skip[None, :] * grad_y
    grads = jnp.stack([grad_o * y_full, grad_mixed * filtered[2], grad_mixed * filtered[1]])
    after = passed_along(grads[:, :rim_width, :], "ctx", -1)
    grads_ext = jnp.concatenate([grads, after], axis=1)
    stream_grads = jnp.zeros((3, seq_rows, width), jnp.float32)
    tap_terms = []
    for j in range(tap_count):
        stream_grads = (
            stream_grads + short_filters[:, j, None, :] * grads_ext[:, j : j + seq_rows, :]
        )
        tap_terms.append(
            jnp.sum(grads * extended[:, rim_width - j : rim_width - j + seq_rows, :], axis=1)
        )
    short_terms = jnp.stack(tap_terms, axis=1)
    skip_term = jnp.sum(grad_y * mixed, axis=0)
    d_short, d_skip = lax.psum((short_terms, skip_term), "ctx")
    return (
        stream_grads[0].astype(jnp.bfloat16),
        stream_grads[1].astype(jnp.bfloat16),
        stream_grads[2].astype(jnp.bfloat16),
        d_long,
        d_short,
        d_skip,
    )


def solution(mesh):
    in_specs = (
        P("ctx", "ch"),
        P("ctx", "ch"),
        P("ctx", "ch"),
        P("ctx", "ch"),
        P(None, None, "ch"),
        P("ch"),
        P("ch", None),
        P("ctx", "ch"),
    )
    out_specs = (
        P("ctx", "ch"),
        P("ctx", "ch"),
        P("ctx", "ch"),
        P("ctx", "ch"),
        P(None, None, "ch"),
        P("ch"),
    )
    return jax.shard_map(
        per_device, mesh=mesh, in_specs=in_specs, out_specs=out_specs, check_vma=False
    )
```

profile of v0, /device:TPU:128, one launch (start us, length us, event | category | flops | bytes accessed | tf_op | source)
XLA Modules:
  0.0 701.8 jit_solution(1200529167491770491)
XLA Ops:
  13.0 4.5 collective-permute-done
  20.2 25.8 %all-gather.2.cloned.1.call-done = bf16[256,8192]{1,0:T(8,128)(2,1)} async-done(((bf16[256,1024]{1,0:T(8,128)(2,1)}), bf16[256,8192]{1,0:T(8,128)(2,1)}) %all-gather.2.cloned.1.call-update) | async-done | bytes 4194320 | tf_op jit(solution)/shard_map/all_gather | solution.py:111
  46.0 7.1 %convolution_convert_fusion = bf16[256,512]{1,0:T(8,128)(2,1)S(1)} fusion(bf16[256,8192]{1,0:T(8,128)(2,1)} %all-gather.2.cloned.1.call-done, bf16[512,8192]{1,0:T(8,128)(2,1)} %param.14), kind=kOutput, calls=%fused_computation.60 | convolution fusion | flops 2147614720 | bytes 12845056 | tf_op jit(solution)/shard_map/dot_general | solution.py:110
  56.1 10.0 %all-to-all-start = ((f32[3,1,256,512]{3,1,0,2:T(1,128)}), f32[3,1,256,512]{3,1,0,2:T(1,128)}, u32[]{:S(2)}, u32[]{:S(2)}) async-start(f32[3,1,256,512]{3,1,0,2:T(1,128)} %copy.56), calls=%async_computation | async-start | bytes 3145728 | tf_op jit(solution)/shard_map/all_to_all | solution.py:119
  66.3 36.3 %all-to-all-done = f32[3,1,256,512]{3,1,0,2:T(1,128)} async-done(((f32[3,1,256,512]{3,1,0,2:T(1,128)}), f32[3,1,256,512]{3,1,0,2:T(1,128)}, u32[]{:S(2)}, u32[]{:S(2)}) %all-to-all-start) | async-done | bytes 1572896 | tf_op jit(solution)/shard_map/all_to_all | solution.py:119
  104.2 4.0 fusion.29
  108.1 4.9 fusion.1
  114.3 4.0 copy.60
  118.4 145.3 %all_to_all.57 = f32[3,2,64,8,512]{4,3,0,1,2:T(8,128)S(1)} all-to-all(f32[3,2,64,8,512]{4,3,0,1,2:T(8,128)S(1)} %copy.60), channel_id=1, replica_groups=mesh['ctx'=32,'ch'=8] {'ctx'}, dimensions={2} | all-to-all | bytes 12582912 | tf_op jit(solution)/shard_map/all_to_all | solution.py:37
  264.8 6.3 fusion.12
  271.1 6.5 fusion.13
  277.5 6.4 subtract_bitcast_fusion.1
  284.0 6.7 add_bitcast_fusion.1
  298.9 4.0 subtract_bitcast_fusion
  310.3 10.3 %copy.65 = f32[3,2,2,256,512]{4,2,0,1,3:T(2,128)} copy(f32[3,2,2,256,512]{3,4,2,0,1:T(8,128)} %pad_maximum_fusion.1) | data formatting | bytes 12582912 | tf_op jit(solution)/shard_map/stack | solution.py:68
  320.6 144.6 %all_to_all.58 = f32[3,2,2,256,512]{4,2,0,1,3:T(2,128)S(1)} all-to-all(f32[3,2,2,256,512]{4,2,0,1,3:T(2,128)} %copy.65), channel_id=1, replica_groups=mesh['ctx'=32,'ch'=8] {'ctx'}, dimensions={3} | all-to-all | bytes 12582912 | tf_op jit(solution)/shard_map/all_to_all | solution.py:67
  465.2 4.6 copy.97
  469.8 10.3 %copy.67 = f32[3,2,32,2,8,512]{5,3,2,4,0,1:T(2,128)} copy(f32[3,2,32,2,8,512]{5,4,2,3,1,0:T(8,128)} %bitcast.217) | data formatting | bytes 12582912 | tf_op jit(solution)/shard_map/all_to_all | solution.py:67
  480.1 8.5 %all_to_all.51 = f32[3,2,64,8,512]{4,2,3,0,1:T(8,128)} reshape(f32[3,2,32,2,8,512]{5,3,2,4,0,1:T(2,128)} %copy.67) | data formatting | bytes 12582912 | tf_op jit(solution)/shard_map/all_to_all | solution.py:67
  488.6 4.5 fusion.4
  493.1 4.6 multiply_bitcast_fusion
  498.6 43.2 %all_to_all.59 = f32[3,32,8,512]{3,2,0,1:T(8,128)S(1)} all-to-all(f32[3,32,8,512]{3,2,0,1:T(8,128)S(1)} %copy.68), channel_id=1, replica_groups=mesh['ctx'=32,'ch'=8] {'ctx'}, dimensions={1} | all-to-all | bytes 3145728 | tf_op jit(solution)/shard_map/all_to_all | solution.py:138
  542.3 4.9 collective-permute-start.1
  549.9 143.3 %all-reduce = (f32[3,3,512]{2,0,1:T(4,128)S(1)}, f32[512]{0:T(512)}) all-reduce(f32[3,3,512]{2,0,1:T(4,128)S(1)} %pad_maximum_fusion.14, f32[512]{0:T(512)S(1)} %get-tuple-element.46), channel_id=1, replica_groups=mesh['ctx'=32,'ch'=8] {'ctx'}, use_global_device_ids=true, to_apply=%region_3.4 | all-reduce | flops 5120 | bytes 40960 | tf_op jit(solution)/shard_map/psum | solution.py:160
  (41 shorter events, 36.5 us)
Async XLA Ops:
  7.2 38.9 %all-gather.2.cloned.1.call-start = ((), (), s32[]{:S(2)}) async-start(), calls=%async_computation.4 | async-start | bytes 4718592 | tf_op jit(solution)/shard_map/all_gather | solution.py:111
  8.6 8.8 %collective-permute-start = (bf16[3,2,512]{2,1,0:T(2,128)(2,1)S(1)}, bf16[3,2,512]{2,1,0:T(2,128)(2,1)S(1)}, u32[]{:S(2)}, u32[]{:S(2)}) collective-permute-start(bf16[3,2,512]{2,1,0:T(2,128)(2,1)S(1)} %pad_maximum_fusion.15), channel_id=1, source_target_pairs={{0,8},{8,16},{16,24},{24,32},{32,40},{40,48},{48,56},{56,64},{64,7... | collective-permute-start | bytes 18440 | tf_op jit(solution)/shard_map/ppermute | solution.py:11
  46.0 7.2 %copy-start = (f32[1,256,512]{2,1,0:T(8,128)S(1)}, f32[1,256,512]{2,1,0:T(8,128)}, u32[]{:S(2)}) copy-start(f32[1,256,512]{2,1,0:T(8,128)} %slice_multiply_fusion.2) | copy-start | bytes 1572868
  46.0 7.2 %copy-start.1 = (f32[256,512]{1,0:T(8,128)S(1)}, f32[256,512]{1,0:T(8,128)}, u32[]{:S(2)}) copy-start(f32[256,512]{1,0:T(8,128)} %param.11) | copy-start | bytes 1572868
  56.1 46.5 %all-to-all-start = ((f32[3,1,256,512]{3,1,0,2:T(1,128)}), f32[3,1,256,512]{3,1,0,2:T(1,128)}, u32[]{:S(2)}, u32[]{:S(2)}) async-start(f32[3,1,256,512]{3,1,0,2:T(1,128)} %copy.56), calls=%async_computation | async-start | bytes 3145728 | tf_op jit(solution)/shard_map/all_to_all | solution.py:119
  497.6 44.2 %copy-start.2 = (f32[512]{0:T(512)S(1)}, f32[512]{0:T(512)}, u32[]{:S(2)}) copy-start(f32[512]{0:T(512)} %param.13) | copy-start | bytes 6148
  542.3 6.3 collective-permute-start.1
Sparse Core Ops, SparseCore 0:
  9.8 36.1 all-gather.1
where the time goes:
time: 707 us; the launch traced here: 702 us
  blocking collectives  477 us (67%)
  waiting for transfers between devices  67.8 us (10%)
  matrix products  66.2 us (9%)
  local copies, waits for them, and re-layouts  47.2 us (7%)
  starting transfers between devices  18.5 us (3%)
  between operations  14.6 us (2%)
  other arithmetic  11 us (2%)
    all_to_all x1, blocking collectives, forward_full(): lax.all_to_all(jnp.stack([second_real, second_imag], axis=1), 'ctx', spli...  145 us
    all_to_all x1, blocking collectives, inverse_full(): lax.all_to_all(jnp.stack([back_real, back_imag], axis=1), 'ctx', split_ax...  145 us
    psum x1, blocking collectives, per_device(): d_short, d_skip = lax.psum((short_terms, skip_term), 'ctx')  143 us
    dot_general x12, matrix products, mat_apply(): return jnp.einsum(form, table, data, precision=lax.Precision.HIGHEST)  59.1 us
    all_to_all x1, blocking collectives, per_device(): lax.all_to_all(result_real, 'ctx', split_axis=1, concat_axis=2, tiled=True)  43.2 us
    all_to_all x1, waiting for transfers between devices, per_device(): lax.all_to_all(signals[:, None], 'ctx', split_axis=2, concat_axis=1, tile...  36.3 us
    all_gather x1, waiting for transfers between devices, per_device(): lax.all_gather(d_out, 'ch', axis=1, tiled=True)  25.8 us
    all_to_all x3, local copies, waits for them, and re-layouts, inverse_full(): lax.all_to_all(jnp.stack([back_real, back_imag], axis=1), 'ctx', split_ax...  23.3 us
  transfers between devices with their start and end apart: 4, of which 4 were waited for; matrix products, arithmetic and copies ran while one was open for 1% of the time, Pallas kernels for 0%

commit v1 on v0

--- a/solution.py
+++ b/solution.py
@@ -64,9 +64,11 @@
     back_imag = mat_apply(fine_cos, spec_imag, "bk,smkc->smbc") + mat_apply(
         fine_sin, spec_real, "bk,smkc->smbc"
     )
-    returned = lax.all_to_all(
-        jnp.stack([back_real, back_imag], axis=1), "ctx", split_axis=3, concat_axis=2, tiled=True
-    )
+    own = jnp.stack([back_real, back_imag], axis=1)
+    devices_2 = lax.axis_size("ctx")
+    pieces = jnp.stack(jnp.split(own, devices_2, axis=3), axis=0)
+    pieces = lax.all_to_all(pieces, "ctx", split_axis=0, concat_axis=0)
+    returned = jnp.concatenate(pieces, axis=2)
     part_real = returned[:, 0]
     part_imag = returned[:, 1]
     freq_coarse = jnp.arange(2 * ctx_size, dtype=jnp.int32)

time: 707 us -> 691 us (0.977)
  local copies, waits for them, and re-layouts: 47.2 us -> 32.1 us
    all_to_all x3 -> x0, local copies, waits for them, and re-layouts: 23.3 us -> none  [inverse_full(): lax.all_to_all(jnp.stack([back_real, back_imag], axis=1), 'ctx', split_ax...]
    reshape x0 -> x2, local copies, waits for them, and re-layouts: none -> 18.7 us  [inverse_full(): returned = jnp.concatenate(pieces, axis=2)]
    another operation x1 -> x0, local copies, waits for them, and re-layouts: 10.3 us -> none  [inverse_full(): jnp.stack([back_real, back_imag], axis=1)]
where the time goes in v1:
time: 691 us; the launch traced here: 685 us
  blocking collectives  476 us (69%)
  waiting for transfers between devices  67.5 us (10%)
  matrix products  67.4 us (10%)
  local copies, waits for them, and re-layouts  32.1 us (5%)
  starting transfers between devices  18.8 us (3%)
  between operations  15 us (2%)
  other arithmetic  8.03 us (1%)
    all_to_all x1, blocking collectives, forward_full(): lax.all_to_all(jnp.stack([second_real, second_imag], axis=1), 'ctx', spli...  145 us
    all_to_all x1, blocking collectives, inverse_full(): pieces = lax.all_to_all(pieces, 'ctx', split_axis=0, concat_axis=0)  145 us
    psum x1, blocking collectives, per_device(): d_short, d_skip = lax.psum((short_terms, skip_term), 'ctx')  143 us
    dot_general x12, matrix products, mat_apply(): return jnp.einsum(form, table, data, precision=lax.Precision.HIGHEST)  60.3 us
    all_to_all x1, blocking collectives, per_device(): lax.all_to_all(result_real, 'ctx', split_axis=1, concat_axis=2, tiled=True)  43 us
    all_to_all x1, waiting for transfers between devices, per_device(): lax.all_to_all(signals[:, None], 'ctx', split_axis=2, concat_axis=1, tile...  36 us
    all_gather x1, waiting for transfers between devices, per_device(): lax.all_gather(d_out, 'ch', axis=1, tiled=True)  25.8 us
    reshape x2, local copies, waits for them, and re-layouts, inverse_full(): returned = jnp.concatenate(pieces, axis=2)  18.7 us
  transfers between devices with their start and end apart: 4, of which 4 were waited for; matrix products, arithmetic and copies ran while one was open for 1% of the time, Pallas kernels for 0%

profile of v1, /device:TPU:128, one launch (start us, length us, event | category | flops | bytes accessed | tf_op | source)
XLA Modules:
  0.0 685.3 jit_solution(293283809649026237)
XLA Ops:
  13.0 4.5 collective-permute-done
  20.2 25.8 %all-gather.2.cloned.1.call-done = bf16[256,8192]{1,0:T(8,128)(2,1)} async-done(((bf16[256,1024]{1,0:T(8,128)(2,1)}), bf16[256,8192]{1,0:T(8,128)(2,1)}) %all-gather.2.cloned.1.call-update) | async-done | bytes 4194320 | tf_op jit(solution)/shard_map/all_gather | solution.py:113
  46.0 7.1 %convolution_convert_fusion = bf16[256,512]{1,0:T(8,128)(2,1)S(1)} fusion(bf16[256,8192]{1,0:T(8,128)(2,1)} %all-gather.2.cloned.1.call-done, bf16[512,8192]{1,0:T(8,128)(2,1)} %param.14), kind=kOutput, calls=%fused_computation.120 | convolution fusion | flops 2147614720 | bytes 12845056 | tf_op jit(solution)/shard_map/dot_general | solution.py:112
  56.1 10.3 %all-to-all-start = ((f32[3,1,256,512]{3,1,0,2:T(1,128)}), f32[3,1,256,512]{3,1,0,2:T(1,128)}, u32[]{:S(2)}, u32[]{:S(2)}) async-start(f32[3,1,256,512]{3,1,0,2:T(1,128)} %copy.67), calls=%async_computation | async-start | bytes 3145728 | tf_op jit(solution)/shard_map/all_to_all | solution.py:121
  66.6 36.0 %all-to-all-done = f32[3,1,256,512]{3,1,0,2:T(1,128)} async-done(((f32[3,1,256,512]{3,1,0,2:T(1,128)}), f32[3,1,256,512]{3,1,0,2:T(1,128)}, u32[]{:S(2)}, u32[]{:S(2)}) %all-to-all-start) | async-done | bytes 1572896 | tf_op jit(solution)/shard_map/all_to_all | solution.py:121
  104.2 4.0 fusion.29
  108.1 5.0 fusion.1
  118.2 145.3 %all_to_all.44 = f32[3,2,64,8,512]{4,3,0,1,2:T(8,128)S(1)} all-to-all(f32[3,2,64,8,512]{4,3,0,1,2:T(8,128)S(1)} %copy.71), channel_id=1, replica_groups=mesh['ctx'=32,'ch'=8] {'ctx'}, dimensions={2} | all-to-all | bytes 12582912 | tf_op jit(solution)/shard_map/all_to_all | solution.py:37
  264.5 6.3 fusion.12
  270.8 6.7 fusion.13
  277.5 6.3 subtract_bitcast_fusion.1
  283.8 6.5 add_bitcast_fusion.1
  291.2 4.1 fusion.16
  295.3 4.1 fusion.17
  299.4 4.1 add_bitcast_fusion
  303.5 4.3 subtract_bitcast_fusion
  308.6 144.8 %all_to_all.45 = f32[32,3,2,2,8,512]{5,4,3,1,2,0:T(8,128)} all-to-all(f32[32,3,2,2,8,512]{5,4,3,1,2,0:T(8,128)S(1)} %fusion.84), channel_id=1, replica_groups=mesh['ctx'=32,'ch'=8] {'ctx'}, dimensions={0} | all-to-all | bytes 12582912 | tf_op jit(solution)/shard_map/all_to_all | solution.py:70
  453.4 10.3 %copy.80 = f32[3,2,32,2,8,512]{5,3,2,4,0,1:T(2,128)} copy(f32[3,2,32,2,8,512]{5,4,3,0,1,2:T(8,128)} %bitcast.279) | data formatting | bytes 12582912 | tf_op jit(solution)/shard_map/reshape | solution.py:71
  463.7 8.5 %reshape.100 = f32[3,2,64,8,512]{4,2,3,0,1:T(8,128)} reshape(f32[3,2,32,2,8,512]{5,3,2,4,0,1:T(2,128)} %copy.80) | data formatting | bytes 12582912 | tf_op jit(solution)/shard_map/reshape | solution.py:71
  472.1 4.5 fusion.4
  476.6 4.6 multiply_bitcast_fusion
  482.1 43.0 %all_to_all.46 = f32[3,32,8,512]{3,2,0,1:T(8,128)S(1)} all-to-all(f32[3,32,8,512]{3,2,0,1:T(8,128)S(1)} %copy.81), channel_id=1, replica_groups=mesh['ctx'=32,'ch'=8] {'ctx'}, dimensions={1} | all-to-all | bytes 3145728 | tf_op jit(solution)/shard_map/all_to_all | solution.py:140
  525.6 5.0 collective-permute-start.1
  533.2 143.3 %all-reduce = (f32[3,3,512]{2,0,1:T(4,128)S(1)}, f32[512]{0:T(512)}) all-reduce(f32[3,3,512]{2,0,1:T(4,128)S(1)} %pad_maximum_fusion.14, f32[512]{0:T(512)S(1)} %get-tuple-element.46), channel_id=1, replica_groups=mesh['ctx'=32,'ch'=8] {'ctx'}, use_global_device_ids=true, to_apply=%region_3.4 | all-reduce | flops 5120 | bytes 40960 | tf_op jit(solution)/shard_map/psum | solution.py:162
  (70 shorter events, 26.1 us)
Async XLA Ops:
  7.2 38.9 %all-gather.2.cloned.1.call-start = ((), (), s32[]{:S(2)}) async-start(), calls=%async_computation.4 | async-start | bytes 4718592 | tf_op jit(solution)/shard_map/all_gather | solution.py:113
  8.6 8.8 %collective-permute-start = (bf16[3,2,512]{2,1,0:T(2,128)(2,1)S(1)}, bf16[3,2,512]{2,1,0:T(2,128)(2,1)S(1)}, u32[]{:S(2)}, u32[]{:S(2)}) collective-permute-start(bf16[3,2,512]{2,1,0:T(2,128)(2,1)S(1)} %pad_maximum_fusion.15), channel_id=1, source_target_pairs={{0,8},{8,16},{16,24},{24,32},{32,40},{40,48},{48,56},{56,64},{64,7... | collective-permute-start | bytes 18440 | tf_op jit(solution)/shard_map/ppermute | solution.py:11
  46.0 7.2 %copy-start = (f32[1,256,512]{2,1,0:T(8,128)S(1)}, f32[1,256,512]{2,1,0:T(8,128)}, u32[]{:S(2)}) copy-start(f32[1,256,512]{2,1,0:T(8,128)} %slice_multiply_fusion.2) | copy-start | bytes 1572868
  46.0 7.2 %copy-start.1 = (f32[256,512]{1,0:T(8,128)S(1)}, f32[256,512]{1,0:T(8,128)}, u32[]{:S(2)}) copy-start(f32[256,512]{1,0:T(8,128)} %param.11) | copy-start | bytes 1572868
  56.1 46.5 %all-to-all-start = ((f32[3,1,256,512]{3,1,0,2:T(1,128)}), f32[3,1,256,512]{3,1,0,2:T(1,128)}, u32[]{:S(2)}, u32[]{:S(2)}) async-start(f32[3,1,256,512]{3,1,0,2:T(1,128)} %copy.67), calls=%async_computation | async-start | bytes 3145728 | tf_op jit(solution)/shard_map/all_to_all | solution.py:121
  481.2 43.9 %copy-start.2 = (f32[512]{0:T(512)S(1)}, f32[512]{0:T(512)}, u32[]{:S(2)}) copy-start(f32[512]{0:T(512)} %param.13) | copy-start | bytes 6148
  525.6 6.4 collective-permute-start.1
Sparse Core Ops, SparseCore 0:
  9.8 36.1 all-gather.1
